TPU v7x, 32 devices: a whole 2x2x4 slice. The times are simulated.
32 devices in a mesh: parts: 2 (over y), span: 4 (over x, core), seq: 4 (over z).
Axes of the slice: x: 2, y: 2, z: 4, core: 2. Of those that a mesh axis runs over, the one named last changes fastest.
Arguments:
- q_in: bfloat16 [8, 1024, 4096], P(('parts', 'span'), 'seq'), parts along dimension 0, may hold values from -9 to 9
- k_in: bfloat16 [8, 1024, 4096], P(('parts', 'span'), 'seq'), parts along dimension 0, may hold values from -9 to 9
- v_in: bfloat16 [8, 1024, 4096], P(('parts', 'span'), 'seq'), parts along dimension 0, may hold values from -18 to 18
- timesteps: int32 [8], P('parts'), parts along dimension 0, may hold values from 0 to 31
- gate_table: float32 [32, 4096], replicated, may hold values from 0.1 to 1.9
Outputs:
- gated_out: bfloat16 [8, 1024, 4096], P(('parts', 'span'), 'seq'), parts along dimension 0
There are 2 independent parts, one for each index of `parts`. A program takes and returns all parts, laid end to end along the dimension named above; an argument that names none is the same for every part. Nothing has to cross between parts.
All inputs are finite; a program needn't handle non-finite values.
Results may differ from a plain program's by a relative error of at most 0.0053.
Values may be sent and summed in bfloat16 or wider, within the bound.
A program may use at most 128 MiB of HBM per device.

v0:
```python
import math
import jax
import jax.numpy as jnp
from jax import lax
from jax.sharding import PartitionSpec as P

HD = 128
masked_score = -1e30


def local(q_in, k_in, v_in, timesteps, gate_table):
    head_rows, key_rows, value_rows = (
        lax.all_to_all(q_in[0], "seq", split_axis=1, concat_axis=0, tiled=True),
        lax.all_to_all(k_in[0], "seq", split_axis=1, concat_axis=0, tiled=True),
        lax.all_to_all(v_in[0], "seq", split_axis=1, concat_axis=0, tiled=True),
    )
    length = head_rows.shape[0]
    columns = head_rows.shape[1]
    heads = columns // HD
    scale = HD ** (-0.5)
    span_id = lax.axis_index("span")
    limit = (span_id + 1) * length
    query_three = head_rows.reshape(length, heads, HD)
    init = (
        jnp.full((heads, length), masked_score, jnp.float32),
        jnp.zeros((heads, length), jnp.float32),
        jnp.zeros((length, heads, HD), jnp.float32),
    )
    key_piece = lax.all_gather(key_rows, "span", axis=0, tiled=True)
    value_piece = lax.all_gather(value_rows, "span", axis=0, tiled=True)
    count = key_piece.shape[0]
    block = math.gcd(count, 512)

    def one_block(index, state):
        top, total, accum = state
        offset = index * block
        key_block = lax.dynamic_slice_in_dim(key_piece, offset, block, 0).reshape(block, heads, HD)
        value_block = lax.dynamic_slice_in_dim(value_piece, offset, block, 0).reshape(
            block, heads, HD
        )
        scores = (
            jnp.einsum("qhd,khd->hqk", query_three, key_block, preferred_element_type=jnp.float32)
            * scale
        )
        keep = offset + jnp.arange(block) < limit
        scores = jnp.where(keep[None, None, :], scores, masked_score)
        new_top = jnp.maximum(top, jnp.max(scores, axis=-1))
        expo = jnp.where(keep[None, None, :], jnp.exp(scores - new_top[:, :, None]), 0.0)
        shrink = jnp.exp(top - new_top)
        total = total * shrink + jnp.sum(expo, axis=-1)
        mixed = jnp.einsum(
            "hqk,khd->qhd",
            expo.astype(jnp.bfloat16),
            value_block,
            preferred_element_type=jnp.float32,
        )
        accum = accum * shrink.T[:, :, None] + mixed
        return (new_top, total, accum)

    def run_blocks(state):
        return lax.fori_loop(0, count // block, one_block, state)

    def keep_state(state):
        return state

    top, total, accum = lax.cond(jnp.int32(0) < limit, run_blocks, keep_state, init)
    attn = (accum / total.T[:, :, None]).reshape(length, columns).astype(jnp.bfloat16)
    token_rows = lax.all_to_all(attn, "seq", split_axis=0, concat_axis=1, tiled=True)
    steps_count = gate_table.shape[0]
    span_step = lax.dynamic_index_in_dim(timesteps, span_id, 0, keepdims=False)
    picked = (jnp.arange(steps_count) == span_step).astype(jnp.float32)
    gate = jnp.dot(picked, gate_table, precision=lax.Precision.HIGHEST)
    return (token_rows.astype(jnp.float32) * gate[None, :]).astype(jnp.bfloat16)[None]


def solution(mesh):
    in_specs = (
        P(("parts", "span"), "seq", None),
        P(("parts", "span"), "seq", None),
        P(("parts", "span"), "seq", None),
        P("parts"),
        P(),
    )
    out_specs = P(("parts", "span"), "seq", None)
    return jax.shard_map(local, mesh=mesh, in_specs=in_specs, out_specs=out_specs, check_vma=False)
```

profile of v0, /device:TPU:0, one launch (start us, length us, event | category | flops | bytes accessed | tf_op | source)
XLA Modules:
  0.0 533.7 jit_solution(13859830746761117424)
XLA Ops:
  10.7 54.5 %all_to_all.64 = bf16[256,4,1024]{0,2,1:T(8,128)(2,1)S(1)} all-to-all(bf16[256,4,1024]{0,2,1:T(8,128)(2,1)} %bitcast.80), channel_id=1, replica_groups=mesh['parts'=2,'span'=4,'seq'=4] {'seq'}, dimensions={1} | all-to-all | bytes 4194304 | tf_op jit(solution)/shard_map/all_to_all | solution.py:14
  71.8 51.0 %all_to_all.65 = bf16[256,4,1024]{0,2,1:T(8,128)(2,1)S(1)} all-to-all(bf16[256,4,1024]{0,2,1:T(8,128)(2,1)} %bitcast.81), channel_id=1, replica_groups=mesh['parts'=2,'span'=4,'seq'=4] {'seq'}, dimensions={1} | all-to-all | bytes 4194304 | tf_op jit(solution)/shard_map/all_to_all | solution.py:15
  132.9 47.3 %all-to-all-done = bf16[256,4,1024]{0,2,1:T(8,128)(2,1)S(1)} async-done(((bf16[256,4,1024]{0,2,1:T(8,128)(2,1)}), bf16[256,4,1024]{0,2,1:T(8,128)(2,1)S(1)}, u32[]{:S(2)}, u32[]{:S(2)}) %all-to-all-start) | async-done | bytes 2097184 | tf_op jit(solution)/shard_map/all_to_all | solution.py:13
  180.2 5.0 all-gather.5.cloned.1.call-done
  185.2 271.6 %conditional.1 = (f32[8,1024]{1,0:T(8,128)}, f32[1024,8,128]{0,2,1:T(8,128)}) conditional(s32[]{:T(128)} %convert_element_type.44, () %tuple.27, (bf16[4,256,1024]{1,2,0:T(8,128)(2,1)S(1)}, s32[]{:T(128)}, bf16[4096,1024]{1,0:T(8,128)(2,1)}, bf16[4096,1024]{1,0:T(8,128)(2,1)}) %tuple.65), branch_computations={%region_0.0_spmd, %region_1.6_spmd} | conditional | flops 2205205504 | bytes 151521616 | solution.py:66
  191.5 265.3 %while.17 = (s32[]{:T(128)}, f32[8,1024]{1,0:T(8,128)S(1)}, f32[8,1024]{1,0:T(8,128)}, f32[1024,8,128]{0,2,1:T(8,128)}, s32[]{:T(128)}, /*index=5*/bf16[4096,102...) while((s32[]{:T(128)}, f32[8,1024]{1,0:T(8,128)S(1)}, ...), condition=%wide.region_5.5_spmd.clone, body=%wide.region_2.4_spmd.clone.sunk | while | flops 2205205504 | bytes 138938576 | solution.py:61
  195.7 9.4 %bitcast_reduce_fusion.2 = (f32[8,1024]{1,0:T(8,128)S(1)}, f32[8,512,1024]{2,1,0:T(8,128)}) fusion(pred[512]{0:T(512)(128)(4,1)S(1)} %add_compare_fusion.2, bf16[512,8,128]{0,2,1:T(8,128)(2,1)S(1)} %bitcast.72, bf16[1024,8,128]{2,0,1:T(8,128)(2,1)} %get-tuple-element.338), kind=kOutput, calls=%fused_computation.1.clone.1 | convolution fusion | flops 1086316544 | bytes 19956224 | tf_op jit(solution)/shard_map/cond/branch_1_fun/while/body/eval_jaxpr/qhd,khd->hqk/dot_general | solution.py:42
  205.6 10.9 %bitcast_add_fusion.2 = f32[1024,8,128]{0,2,1:T(8,128)} fusion(f32[1024,8,128]{0,2,1:T(8,128)} %get-tuple-element.323, bf16[512,8,128]{0,2,1:T(8,128)(2,1)S(1)} %bitcast.73, f32[8,512,1024]{2,1,0:T(8,128)} %get-tuple-element.305, f32[8,1024]{1,0:T(8,128)S(1)} %get-tuple-element.333, pred[512]{0:T(512)(128)(4,1)S(1)} %add_compare_fusion.2, ...), kind=kOutput, calls=%fused_computation.10.clone.1 | convolution fusion | flops 1097859072 | bytes 26280448 | tf_op jit(solution)/shard_map/cond/branch_1_fun/while/body/eval_jaxpr/hqk,khd->qhd/dot_general | solution.py:51
  217.7 4.6 fusion.37
  227.1 9.4 %bitcast_reduce_fusion.2 = (f32[8,1024]{1,0:T(8,128)S(1)}, f32[8,512,1024]{2,1,0:T(8,128)}) fusion(pred[512]{0:T(512)(128)(4,1)S(1)} %add_compare_fusion.2, bf16[512,8,128]{0,2,1:T(8,128)(2,1)S(1)} %bitcast.72, bf16[1024,8,128]{2,0,1:T(8,128)(2,1)} %get-tuple-element.338), kind=kOutput, calls=%fused_computation.1.clone.1 | convolution fusion | flops 1086316544 | bytes 19956224 | tf_op jit(solution)/shard_map/cond/branch_1_fun/while/body/eval_jaxpr/qhd,khd->hqk/dot_general | solution.py:42
  237.1 12.1 %bitcast_add_fusion.2 = f32[1024,8,128]{0,2,1:T(8,128)} fusion(f32[1024,8,128]{0,2,1:T(8,128)} %get-tuple-element.323, bf16[512,8,128]{0,2,1:T(8,128)(2,1)S(1)} %bitcast.73, f32[8,512,1024]{2,1,0:T(8,128)} %get-tuple-element.305, f32[8,1024]{1,0:T(8,128)S(1)} %get-tuple-element.333, pred[512]{0:T(512)(128)(4,1)S(1)} %add_compare_fusion.2, ...), kind=kOutput, calls=%fused_computation.10.clone.1 | convolution fusion | flops 1097859072 | bytes 26280448 | tf_op jit(solution)/shard_map/cond/branch_1_fun/while/body/eval_jaxpr/hqk,khd->qhd/dot_general | solution.py:51
  250.3 4.6 fusion.37
  260.5 9.4 %bitcast_reduce_fusion.2 = (f32[8,1024]{1,0:T(8,128)S(1)}, f32[8,512,1024]{2,1,0:T(8,128)}) fusion(pred[512]{0:T(512)(128)(4,1)S(1)} %add_compare_fusion.2, bf16[512,8,128]{0,2,1:T(8,128)(2,1)S(1)} %bitcast.72, bf16[1024,8,128]{2,0,1:T(8,128)(2,1)} %get-tuple-element.338), kind=kOutput, calls=%fused_computation.1.clone.1 | convolution fusion | flops 1086316544 | bytes 19956224 | tf_op jit(solution)/shard_map/cond/branch_1_fun/while/body/eval_jaxpr/qhd,khd->hqk/dot_general | solution.py:42
  270.5 12.1 %bitcast_add_fusion.2 = f32[1024,8,128]{0,2,1:T(8,128)} fusion(f32[1024,8,128]{0,2,1:T(8,128)} %get-tuple-element.323, bf16[512,8,128]{0,2,1:T(8,128)(2,1)S(1)} %bitcast.73, f32[8,512,1024]{2,1,0:T(8,128)} %get-tuple-element.305, f32[8,1024]{1,0:T(8,128)S(1)} %get-tuple-element.333, pred[512]{0:T(512)(128)(4,1)S(1)} %add_compare_fusion.2, ...), kind=kOutput, calls=%fused_computation.10.clone.1 | convolution fusion | flops 1097859072 | bytes 26280448 | tf_op jit(solution)/shard_map/cond/branch_1_fun/while/body/eval_jaxpr/hqk,khd->qhd/dot_general | solution.py:51
  283.7 4.6 fusion.37
  293.9 9.4 %bitcast_reduce_fusion.2 = (f32[8,1024]{1,0:T(8,128)S(1)}, f32[8,512,1024]{2,1,0:T(8,128)}) fusion(pred[512]{0:T(512)(128)(4,1)S(1)} %add_compare_fusion.2, bf16[512,8,128]{0,2,1:T(8,128)(2,1)S(1)} %bitcast.72, bf16[1024,8,128]{2,0,1:T(8,128)(2,1)} %get-tuple-element.338), kind=kOutput, calls=%fused_computation.1.clone.1 | convolution fusion | flops 1086316544 | bytes 19956224 | tf_op jit(solution)/shard_map/cond/branch_1_fun/while/body/eval_jaxpr/qhd,khd->hqk/dot_general | solution.py:42
  303.9 12.1 %bitcast_add_fusion.2 = f32[1024,8,128]{0,2,1:T(8,128)} fusion(f32[1024,8,128]{0,2,1:T(8,128)} %get-tuple-element.323, bf16[512,8,128]{0,2,1:T(8,128)(2,1)S(1)} %bitcast.73, f32[8,512,1024]{2,1,0:T(8,128)} %get-tuple-element.305, f32[8,1024]{1,0:T(8,128)S(1)} %get-tuple-element.333, pred[512]{0:T(512)(128)(4,1)S(1)} %add_compare_fusion.2, ...), kind=kOutput, calls=%fused_computation.10.clone.1 | convolution fusion | flops 1097859072 | bytes 26280448 | tf_op jit(solution)/shard_map/cond/branch_1_fun/while/body/eval_jaxpr/hqk,khd->qhd/dot_general | solution.py:51
  317.1 4.6 fusion.37
  327.4 9.4 %bitcast_reduce_fusion.2 = (f32[8,1024]{1,0:T(8,128)S(1)}, f32[8,512,1024]{2,1,0:T(8,128)}) fusion(pred[512]{0:T(512)(128)(4,1)S(1)} %add_compare_fusion.2, bf16[512,8,128]{0,2,1:T(8,128)(2,1)S(1)} %bitcast.72, bf16[1024,8,128]{2,0,1:T(8,128)(2,1)} %get-tuple-element.338), kind=kOutput, calls=%fused_computation.1.clone.1 | convolution fusion | flops 1086316544 | bytes 19956224 | tf_op jit(solution)/shard_map/cond/branch_1_fun/while/body/eval_jaxpr/qhd,khd->hqk/dot_general | solution.py:42
  337.3 12.1 %bitcast_add_fusion.2 = f32[1024,8,128]{0,2,1:T(8,128)} fusion(f32[1024,8,128]{0,2,1:T(8,128)} %get-tuple-element.323, bf16[512,8,128]{0,2,1:T(8,128)(2,1)S(1)} %bitcast.73, f32[8,512,1024]{2,1,0:T(8,128)} %get-tuple-element.305, f32[8,1024]{1,0:T(8,128)S(1)} %get-tuple-element.333, pred[512]{0:T(512)(128)(4,1)S(1)} %add_compare_fusion.2, ...), kind=kOutput, calls=%fused_computation.10.clone.1 | convolution fusion | flops 1097859072 | bytes 26280448 | tf_op jit(solution)/shard_map/cond/branch_1_fun/while/body/eval_jaxpr/hqk,khd->qhd/dot_general | solution.py:51
  350.5 4.6 fusion.37
  360.8 9.4 %bitcast_reduce_fusion.2 = (f32[8,1024]{1,0:T(8,128)S(1)}, f32[8,512,1024]{2,1,0:T(8,128)}) fusion(pred[512]{0:T(512)(128)(4,1)S(1)} %add_compare_fusion.2, bf16[512,8,128]{0,2,1:T(8,128)(2,1)S(1)} %bitcast.72, bf16[1024,8,128]{2,0,1:T(8,128)(2,1)} %get-tuple-element.338), kind=kOutput, calls=%fused_computation.1.clone.1 | convolution fusion | flops 1086316544 | bytes 19956224 | tf_op jit(solution)/shard_map/cond/branch_1_fun/while/body/eval_jaxpr/qhd,khd->hqk/dot_general | solution.py:42
  370.7 12.1 %bitcast_add_fusion.2 = f32[1024,8,128]{0,2,1:T(8,128)} fusion(f32[1024,8,128]{0,2,1:T(8,128)} %get-tuple-element.323, bf16[512,8,128]{0,2,1:T(8,128)(2,1)S(1)} %bitcast.73, f32[8,512,1024]{2,1,0:T(8,128)} %get-tuple-element.305, f32[8,1024]{1,0:T(8,128)S(1)} %get-tuple-element.333, pred[512]{0:T(512)(128)(4,1)S(1)} %add_compare_fusion.2, ...), kind=kOutput, calls=%fused_computation.10.clone.1 | convolution fusion | flops 1097859072 | bytes 26280448 | tf_op jit(solution)/shard_map/cond/branch_1_fun/while/body/eval_jaxpr/hqk,khd->qhd/dot_general | solution.py:51
  383.9 4.6 fusion.37
  394.2 9.4 %bitcast_reduce_fusion.2 = (f32[8,1024]{1,0:T(8,128)S(1)}, f32[8,512,1024]{2,1,0:T(8,128)}) fusion(pred[512]{0:T(512)(128)(4,1)S(1)} %add_compare_fusion.2, bf16[512,8,128]{0,2,1:T(8,128)(2,1)S(1)} %bitcast.72, bf16[1024,8,128]{2,0,1:T(8,128)(2,1)} %get-tuple-element.338), kind=kOutput, calls=%fused_computation.1.clone.1 | convolution fusion | flops 1086316544 | bytes 19956224 | tf_op jit(solution)/shard_map/cond/branch_1_fun/while/body/eval_jaxpr/qhd,khd->hqk/dot_general | solution.py:42
  404.1 12.1 %bitcast_add_fusion.2 = f32[1024,8,128]{0,2,1:T(8,128)} fusion(f32[1024,8,128]{0,2,1:T(8,128)} %get-tuple-element.323, bf16[512,8,128]{0,2,1:T(8,128)(2,1)S(1)} %bitcast.73, f32[8,512,1024]{2,1,0:T(8,128)} %get-tuple-element.305, f32[8,1024]{1,0:T(8,128)S(1)} %get-tuple-element.333, pred[512]{0:T(512)(128)(4,1)S(1)} %add_compare_fusion.2, ...), kind=kOutput, calls=%fused_computation.10.clone.1 | convolution fusion | flops 1097859072 | bytes 26280448 | tf_op jit(solution)/shard_map/cond/branch_1_fun/while/body/eval_jaxpr/hqk,khd->qhd/dot_general | solution.py:51
  417.4 4.6 fusion.37
  427.6 9.4 %bitcast_reduce_fusion.2 = (f32[8,1024]{1,0:T(8,128)S(1)}, f32[8,512,1024]{2,1,0:T(8,128)}) fusion(pred[512]{0:T(512)(128)(4,1)S(1)} %add_compare_fusion.2, bf16[512,8,128]{0,2,1:T(8,128)(2,1)S(1)} %bitcast.72, bf16[1024,8,128]{2,0,1:T(8,128)(2,1)} %get-tuple-element.338), kind=kOutput, calls=%fused_computation.1.clone.1 | convolution fusion | flops 1086316544 | bytes 19956224 | tf_op jit(solution)/shard_map/cond/branch_1_fun/while/body/eval_jaxpr/qhd,khd->hqk/dot_general | solution.py:42
  437.5 12.1 %bitcast_add_fusion.2 = f32[1024,8,128]{0,2,1:T(8,128)} fusion(f32[1024,8,128]{0,2,1:T(8,128)} %get-tuple-element.323, bf16[512,8,128]{0,2,1:T(8,128)(2,1)S(1)} %bitcast.73, f32[8,512,1024]{2,1,0:T(8,128)} %get-tuple-element.305, f32[8,1024]{1,0:T(8,128)S(1)} %get-tuple-element.333, pred[512]{0:T(512)(128)(4,1)S(1)} %add_compare_fusion.2, ...), kind=kOutput, calls=%fused_computation.10.clone.1 | convolution fusion | flops 1097859072 | bytes 26280448 | tf_op jit(solution)/shard_map/cond/branch_1_fun/while/body/eval_jaxpr/hqk,khd->qhd/dot_general | solution.py:51
  450.8 4.6 fusion.37
  466.7 4.6 all-to-all-start.3
  472.8 47.3 %all-to-all-done.3 = bf16[4,256,1024]{2,1,0:T(8,128)(2,1)} async-done(((bf16[4,256,1024]{2,1,0:T(8,128)(2,1)}), bf16[4,256,1024]{2,1,0:T(8,128)(2,1)}, u32[]{:S(2)}, u32[]{:S(2)}) %all-to-all-start.3) | async-done | bytes 2097184 | tf_op jit(solution)/shard_map/all_to_all | solution.py:68
  (102 shorter events, 103.1 us)
Async XLA Ops:
  6.5 465.3 %copy-start = (f32[32,4096]{1,0:T(8,128)S(1)}, f32[32,4096]{1,0:T(8,128)}, u32[]{:S(2)}) copy-start(f32[32,4096]{1,0:T(8,128)} %param.13) | copy-start | bytes 1572868
  6.5 173.7 %all-gather.3.cloned.1.call-start = ((), (), s32[]{:S(2)}) async-start(), calls=%async_computation.4 | async-start | bytes 10485760 | tf_op jit(solution)/shard_map/all_gather | solution.py:29
  67.7 117.5 %all-gather.5.cloned.1.call-start = ((), (), s32[]{:S(2)}) async-start(), calls=%async_computation.5 | async-start | bytes 10485760 | tf_op jit(solution)/shard_map/all_gather | solution.py:30
  129.3 50.9 %all-to-all-start = ((bf16[256,4,1024]{0,2,1:T(8,128)(2,1)}), bf16[256,4,1024]{0,2,1:T(8,128)(2,1)S(1)}, u32[]{:S(2)}, u32[]{:S(2)}) async-start(bf16[256,4,1024]{0,2,1:T(8,128)(2,1)} %bitcast.78), calls=%async_computation | async-start | bytes 4194304 | tf_op jit(solution)/shard_map/all_to_all | solution.py:13
  205.6 12.1 %copy-start.1 = (f32[8,512,1024]{2,1,0:T(8,128)S(1)}, f32[8,512,1024]{2,1,0:T(8,128)}, u32[]{:S(2)}) copy-start(f32[8,512,1024]{2,1,0:T(8,128)} %get-tuple-element.305) | copy-start | bytes 50331652 | tf_op jit(solution)/shard_map/cond/branch_1_fun/while
  237.1 13.3 %copy-start.1 = (f32[8,512,1024]{2,1,0:T(8,128)S(1)}, f32[8,512,1024]{2,1,0:T(8,128)}, u32[]{:S(2)}) copy-start(f32[8,512,1024]{2,1,0:T(8,128)} %get-tuple-element.305) | copy-start | bytes 50331652 | tf_op jit(solution)/shard_map/cond/branch_1_fun/while
  270.5 13.3 %copy-start.1 = (f32[8,512,1024]{2,1,0:T(8,128)S(1)}, f32[8,512,1024]{2,1,0:T(8,128)}, u32[]{:S(2)}) copy-start(f32[8,512,1024]{2,1,0:T(8,128)} %get-tuple-element.305) | copy-start | bytes 50331652 | tf_op jit(solution)/shard_map/cond/branch_1_fun/while
  303.9 13.3 %copy-start.1 = (f32[8,512,1024]{2,1,0:T(8,128)S(1)}, f32[8,512,1024]{2,1,0:T(8,128)}, u32[]{:S(2)}) copy-start(f32[8,512,1024]{2,1,0:T(8,128)} %get-tuple-element.305) | copy-start | bytes 50331652 | tf_op jit(solution)/shard_map/cond/branch_1_fun/while
  337.3 13.3 %copy-start.1 = (f32[8,512,1024]{2,1,0:T(8,128)S(1)}, f32[8,512,1024]{2,1,0:T(8,128)}, u32[]{:S(2)}) copy-start(f32[8,512,1024]{2,1,0:T(8,128)} %get-tuple-element.305) | copy-start | bytes 50331652 | tf_op jit(solution)/shard_map/cond/branch_1_fun/while
  370.7 13.3 %copy-start.1 = (f32[8,512,1024]{2,1,0:T(8,128)S(1)}, f32[8,512,1024]{2,1,0:T(8,128)}, u32[]{:S(2)}) copy-start(f32[8,512,1024]{2,1,0:T(8,128)} %get-tuple-element.305) | copy-start | bytes 50331652 | tf_op jit(solution)/shard_map/cond/branch_1_fun/while
  404.1 13.3 %copy-start.1 = (f32[8,512,1024]{2,1,0:T(8,128)S(1)}, f32[8,512,1024]{2,1,0:T(8,128)}, u32[]{:S(2)}) copy-start(f32[8,512,1024]{2,1,0:T(8,128)} %get-tuple-element.305) | copy-start | bytes 50331652 | tf_op jit(solution)/shard_map/cond/branch_1_fun/while
  437.5 13.3 %copy-start.1 = (f32[8,512,1024]{2,1,0:T(8,128)S(1)}, f32[8,512,1024]{2,1,0:T(8,128)}, u32[]{:S(2)}) copy-start(f32[8,512,1024]{2,1,0:T(8,128)} %get-tuple-element.305) | copy-start | bytes 50331652 | tf_op jit(solution)/shard_map/cond/branch_1_fun/while
  462.4 8.9 %copy-start.2 = (s32[4]{0:T(128)S(1)}, s32[4]{0:T(128)}, u32[]{:S(2)}) copy-start(s32[4]{0:T(128)} %param.12) | copy-start | bytes 52
  466.7 53.4 %all-to-all-start.3 = ((bf16[4,256,1024]{2,1,0:T(8,128)(2,1)}), bf16[4,256,1024]{2,1,0:T(8,128)(2,1)}, u32[]{:S(2)}, u32[]{:S(2)}) async-start(bf16[4,256,1024]{2,1,0:T(8,128)(2,1)} %copy.42), calls=%async_computation.3 | async-start | bytes 4194304 | tf_op jit(solution)/shard_map/all_to_all | solution.py:68
Sparse Core Ops, SparseCore 0:
  67.8 57.4 all-gather.2
  126.9 58.2 all-gather.4
where the time goes:
time: 536 us; the launch traced here: 534 us
  matrix products  171 us (32%)
  blocking collectives  105 us (20%)
  waiting for transfers between devices  99.6 us (19%)
  local copies, waits for them, and re-layouts  84 us (16%)
  other arithmetic  51.5 us (10%)
  between operations  13.5 us (3%)
  starting transfers between devices  8.25 us (2%)
    dot_general x8, matrix products, one_block(): jnp.einsum('hqk,khd->qhd', expo.astype(jnp.bfloat16), value_block, prefer...  95.3 us
    dot_general x8, matrix products, one_block(): jnp.einsum('qhd,khd->hqk', query_three, key_block, preferred_element_type...  74.9 us
    all_to_all x1, blocking collectives, local(): lax.all_to_all(k_in[0], 'seq', split_axis=1, concat_axis=0, tiled=True)  54.5 us
    all_to_all x1, blocking collectives, local(): lax.all_to_all(v_in[0], 'seq', split_axis=1, concat_axis=0, tiled=True)  51 us
    all_to_all x1, waiting for transfers between devices, local(): lax.all_to_all(q_in[0], 'seq', split_axis=1, concat_axis=0, tiled=True)  47.3 us
    all_to_all x1, waiting for transfers between devices, local(): lax.all_to_all(attn, 'seq', split_axis=0, concat_axis=1, tiled=True)  47.3 us
    reduce_sum x8, other arithmetic, one_block(): total = total * shrink + jnp.sum(expo, axis=-1)  37 us
    dynamic_slice x16, local copies, waits for them, and re-layouts, one_block(): lax.dynamic_slice_in_dim(value_piece, offset, block, 0)  25.8 us
  transfers between devices with their start and end apart: 4, of which 3 were waited for; matrix products, arithmetic and copies ran while one was open for 2% of the time, Pallas kernels for 0%

commit v1 on v0

--- a/solution.py
+++ b/solution.py
@@ -6,6 +6,29 @@
 
 HD = 128
 masked_score = -1e30
+
+
+def split_up(x, dim, size):
+    before, after = (x.shape[:dim], x.shape[dim + 1 :])
+    return jnp.moveaxis(x.reshape(*before, size, -1, *after), dim, 0)
+
+
+def laid_out(blocks, dim):
+    shape = list(blocks.shape[1:])
+    shape[dim] *= blocks.shape[0]
+    return jnp.moveaxis(blocks, 0, dim).reshape(shape)
+
+
+def sent_to_each(shard, axis, split_dim, concat_dim):
+    peers, index = (lax.axis_size(axis), lax.axis_index(axis))
+    tiles = split_up(shard, split_dim, peers)
+    whole = tiles
+    for step in range(1, peers):
+        target, source = ((index + step) % peers, (index - step) % peers)
+        sent = lax.dynamic_index_in_dim(tiles, target, 0)
+        other = lax.ppermute(sent, axis, [(i, (i + step) % peers) for i in range(peers)])
+        whole = lax.dynamic_update_slice_in_dim(whole, other, source, axis=0)
+    return laid_out(whole, concat_dim)
 
 
 def local(q_in, k_in, v_in, timesteps, gate_table):
@@ -65,7 +88,7 @@
 
     top, total, accum = lax.cond(jnp.int32(0) < limit, run_blocks, keep_state, init)
     attn = (accum / total.T[:, :, None]).reshape(length, columns).astype(jnp.bfloat16)
-    token_rows = lax.all_to_all(attn, "seq", split_axis=0, concat_axis=1, tiled=True)
+    token_rows = sent_to_each(attn, "seq", 0, 1)
     steps_count = gate_table.shape[0]
     span_step = lax.dynamic_index_in_dim(timesteps, span_id, 0, keepdims=False)
     picked = (jnp.arange(steps_count) == span_step).astype(jnp.float32)

time: 536 us -> 566 us (1.056); the launches traced: 534 us -> 555 us
  other arithmetic: 51.5 us -> 84.2 us
  matrix products: 171 us -> 186 us
  local copies, waits for them, and re-layouts: 84 us -> 69.9 us
  waiting for transfers between devices: 99.6 us -> 88.2 us
    all_to_all x1 -> x0, waiting for transfers between devices: 47.3 us -> none  [local(): lax.all_to_all(attn, 'seq', split_axis=0, concat_axis=1, tiled=True)]
    ppermute x0 -> x3, waiting for transfers between devices: none -> 35.9 us  [sent_to_each(): lax.ppermute(sent, axis, [(i, (i + step) % peers) for i in range(peers)])]
    reduce_sum x8, other arithmetic: 37 us -> 65.9 us  [one_block(): total = total * shrink + jnp.sum(expo, axis=-1)]
    dot_general x8, matrix products: 74.9 us -> 91.7 us  [one_block(): jnp.einsum('qhd,khd->hqk', query_three, key_block, preferred_element_type...]
    while x24 -> x8, local copies, waits for them, and re-layouts: 9.48 us -> 0.03 us
    dynamic_slice x16, local copies, waits for them, and re-layouts: 25.8 us -> 18 us  [one_block(): lax.dynamic_slice_in_dim(value_piece, offset, block, 0)]
  transfers between devices with their start and end apart: 4 -> 6, of which waited for: 3 -> 4; matrix products, arithmetic and copies ran while one was open for 2% -> 2% of each run, Pallas kernels for 0% -> 0%
where the time goes in v1:
time: 566 us; the launch traced here: 555 us
  matrix products  186 us (33%)
  blocking collectives  105 us (19%)
  waiting for transfers between devices  88.2 us (16%)
  other arithmetic  84.2 us (15%)
  local copies, waits for them, and re-layouts  69.9 us (12%)
  between operations  13.5 us (2%)
  starting transfers between devices  7.2 us (1%)
    dot_general x8, matrix products, one_block(): jnp.einsum('hqk,khd->qhd', expo.astype(jnp.bfloat16), value_block, prefer...  93.6 us
    dot_general x8, matrix products, one_block(): jnp.einsum('qhd,khd->hqk', query_three, key_block, preferred_element_type...  91.7 us
    reduce_sum x8, other arithmetic, one_block(): total = total * shrink + jnp.sum(expo, axis=-1)  65.9 us
    all_to_all x1, blocking collectives, local(): lax.all_to_all(k_in[0], 'seq', split_axis=1, concat_axis=0, tiled=True)  54.5 us
    all_to_all x1, blocking collectives, local(): lax.all_to_all(v_in[0], 'seq', split_axis=1, concat_axis=0, tiled=True)  51 us
    all_to_all x1, waiting for transfers between devices, local(): lax.all_to_all(q_in[0], 'seq', split_axis=1, concat_axis=0, tiled=True)  47.3 us
    ppermute x3, waiting for transfers between devices, sent_to_each(): lax.ppermute(sent, axis, [(i, (i + step) % peers) for i in range(peers)])  35.9 us
    dynamic_slice x16, local copies, waits for them, and re-layouts, one_block(): lax.dynamic_slice_in_dim(value_piece, offset, block, 0)  18 us
  transfers between devices with their start and end apart: 6, of which 4 were waited for; matrix products, arithmetic and copies ran while one was open for 2% of the time, Pallas kernels for 0%

profile of v1, /device:TPU:0, one launch (start us, length us, event | category | flops | bytes accessed | tf_op | source)
XLA Modules:
  0.0 555.0 jit_solution(18159525951053642551)
XLA Ops:
  10.7 54.5 %all_to_all.54 = bf16[256,4,1024]{0,2,1:T(8,128)(2,1)S(1)} all-to-all(bf16[256,4,1024]{0,2,1:T(8,128)(2,1)} %bitcast.78), channel_id=1, replica_groups=mesh['parts'=2,'span'=4,'seq'=4] {'seq'}, dimensions={1} | all-to-all | bytes 4194304 | tf_op jit(solution)/shard_map/all_to_all | solution.py:37
  71.8 51.0 %all_to_all.55 = bf16[256,4,1024]{0,2,1:T(8,128)(2,1)S(1)} all-to-all(bf16[256,4,1024]{0,2,1:T(8,128)(2,1)} %bitcast.79), channel_id=1, replica_groups=mesh['parts'=2,'span'=4,'seq'=4] {'seq'}, dimensions={1} | all-to-all | bytes 4194304 | tf_op jit(solution)/shard_map/all_to_all | solution.py:38
  132.9 47.3 %all-to-all-done = bf16[256,4,1024]{0,2,1:T(8,128)(2,1)S(1)} async-done(((bf16[256,4,1024]{0,2,1:T(8,128)(2,1)}), bf16[256,4,1024]{0,2,1:T(8,128)(2,1)S(1)}, u32[]{:S(2)}, u32[]{:S(2)}) %all-to-all-start) | async-done | bytes 2097184 | tf_op jit(solution)/shard_map/all_to_all | solution.py:36
  185.2 297.0 %conditional.1 = (f32[8,1024]{1,0:T(8,128)}, f32[1024,8,128]{0,2,1:T(8,128)}) conditional(s32[]{:T(128)} %convert_element_type.44, () %tuple.27, (bf16[4,256,1024]{1,2,0:T(8,128)(2,1)S(1)}, s32[]{:T(128)}, bf16[4096,1024]{1,0:T(8,128)(2,1)}, bf16[4096,1024]{1,0:T(8,128)(2,1)}) %tuple.69), branch_computations={%region_0.0_spmd, %region_1.6_spmd} | conditional | flops 2205205504 | bytes 84412728 | solution.py:89
  191.5 290.8 %while.17 = (s32[]{:T(128)}, f32[8,1024]{1,0:T(8,128)S(1)}, f32[8,1024]{1,0:T(8,128)}, f32[1024,8,128]{0,2,1:T(8,128)}, s32[]{:T(128)}, /*index=5*/bf16[4096,102...) while((s32[]{:T(128)}, f32[8,1024]{1,0:T(8,128)S(1)}, ...), condition=%wide.region_5.5_spmd.clone, body=%wide.region_2.4_spmd.clone.sunk | while | flops 2205205504 | bytes 71829696 | solution.py:84
  194.5 11.5 %bitcast_reduce_fusion.2 = (f32[8,1024]{1,0:T(8,128)S(1)}, f32[8,512,1024]{2,1,0:T(8,128)}) fusion(pred[512]{0:T(512)(128)(4,1)S(1)} %add_compare_fusion.2, bf16[512,8,128]{0,2,1:T(8,128)(2,1)} %bitcast.71, bf16[1024,8,128]{2,0,1:T(8,128)(2,1)} %get-tuple-element.353), kind=kOutput, calls=%fused_computation.1.clone.1 | convolution fusion | flops 1086316544 | bytes 19956224 | tf_op jit(solution)/shard_map/cond/branch_1_fun/while/body/eval_jaxpr/qhd,khd->hqk/dot_general | solution.py:65
  206.0 8.2 %fusion.37 = f32[8,1024]{1,0:T(8,128)S(1)} fusion(f32[8,512,1024]{2,1,0:T(8,128)} %get-tuple-element.320, f32[8,1024]{1,0:T(8,128)S(1)} %get-tuple-element.348, pred[512]{0:T(512)(128)(4,1)S(1)} %add_compare_fusion.2), kind=kLoop, calls=%fused_computation.6.clone.1 | loop fusion | flops 20963328 | bytes 16843264 | tf_op jit(solution)/shard_map/cond/branch_1_fun/while/body/eval_jaxpr/reduce_sum | solution.py:73
  215.5 10.7 %bitcast_add_fusion.2 = f32[1024,8,128]{0,2,1:T(8,128)} fusion(f32[1024,8,128]{0,2,1:T(8,128)} %get-tuple-element.338, bf16[512,8,128]{0,2,1:T(8,128)(2,1)S(1)} %bitcast.72, f32[8,512,1024]{2,1,0:T(8,128)} %get-tuple-element.320, f32[8,1024]{1,0:T(8,128)S(1)} %get-tuple-element.348, pred[512]{0:T(512)(128)(4,1)S(1)} %add_compare_fusion.2, ...), kind=kOutput, calls=%fused_computation.10.clone.1 | convolution fusion | flops 1097859072 | bytes 26280448 | tf_op jit(solution)/shard_map/cond/branch_1_fun/while/body/eval_jaxpr/hqk,khd->qhd/dot_general | solution.py:74
  229.2 11.5 %bitcast_reduce_fusion.2 = (f32[8,1024]{1,0:T(8,128)S(1)}, f32[8,512,1024]{2,1,0:T(8,128)}) fusion(pred[512]{0:T(512)(128)(4,1)S(1)} %add_compare_fusion.2, bf16[512,8,128]{0,2,1:T(8,128)(2,1)} %bitcast.71, bf16[1024,8,128]{2,0,1:T(8,128)(2,1)} %get-tuple-element.353), kind=kOutput, calls=%fused_computation.1.clone.1 | convolution fusion | flops 1086316544 | bytes 19956224 | tf_op jit(solution)/shard_map/cond/branch_1_fun/while/body/eval_jaxpr/qhd,khd->hqk/dot_general | solution.py:65
  240.7 8.2 %fusion.37 = f32[8,1024]{1,0:T(8,128)S(1)} fusion(f32[8,512,1024]{2,1,0:T(8,128)} %get-tuple-element.320, f32[8,1024]{1,0:T(8,128)S(1)} %get-tuple-element.348, pred[512]{0:T(512)(128)(4,1)S(1)} %add_compare_fusion.2), kind=kLoop, calls=%fused_computation.6.clone.1 | loop fusion | flops 20963328 | bytes 16843264 | tf_op jit(solution)/shard_map/cond/branch_1_fun/while/body/eval_jaxpr/reduce_sum | solution.py:73
  250.9 11.8 %bitcast_add_fusion.2 = f32[1024,8,128]{0,2,1:T(8,128)} fusion(f32[1024,8,128]{0,2,1:T(8,128)} %get-tuple-element.338, bf16[512,8,128]{0,2,1:T(8,128)(2,1)S(1)} %bitcast.72, f32[8,512,1024]{2,1,0:T(8,128)} %get-tuple-element.320, f32[8,1024]{1,0:T(8,128)S(1)} %get-tuple-element.348, pred[512]{0:T(512)(128)(4,1)S(1)} %add_compare_fusion.2, ...), kind=kOutput, calls=%fused_computation.10.clone.1 | convolution fusion | flops 1097859072 | bytes 26280448 | tf_op jit(solution)/shard_map/cond/branch_1_fun/while/body/eval_jaxpr/hqk,khd->qhd/dot_general | solution.py:74
  265.8 11.5 %bitcast_reduce_fusion.2 = (f32[8,1024]{1,0:T(8,128)S(1)}, f32[8,512,1024]{2,1,0:T(8,128)}) fusion(pred[512]{0:T(512)(128)(4,1)S(1)} %add_compare_fusion.2, bf16[512,8,128]{0,2,1:T(8,128)(2,1)} %bitcast.71, bf16[1024,8,128]{2,0,1:T(8,128)(2,1)} %get-tuple-element.353), kind=kOutput, calls=%fused_computation.1.clone.1 | convolution fusion | flops 1086316544 | bytes 19956224 | tf_op jit(solution)/shard_map/cond/branch_1_fun/while/body/eval_jaxpr/qhd,khd->hqk/dot_general | solution.py:65
  277.3 8.2 %fusion.37 = f32[8,1024]{1,0:T(8,128)S(1)} fusion(f32[8,512,1024]{2,1,0:T(8,128)} %get-tuple-element.320, f32[8,1024]{1,0:T(8,128)S(1)} %get-tuple-element.348, pred[512]{0:T(512)(128)(4,1)S(1)} %add_compare_fusion.2), kind=kLoop, calls=%fused_computation.6.clone.1 | loop fusion | flops 20963328 | bytes 16843264 | tf_op jit(solution)/shard_map/cond/branch_1_fun/while/body/eval_jaxpr/reduce_sum | solution.py:73
  287.4 11.8 %bitcast_add_fusion.2 = f32[1024,8,128]{0,2,1:T(8,128)} fusion(f32[1024,8,128]{0,2,1:T(8,128)} %get-tuple-element.338, bf16[512,8,128]{0,2,1:T(8,128)(2,1)S(1)} %bitcast.72, f32[8,512,1024]{2,1,0:T(8,128)} %get-tuple-element.320, f32[8,1024]{1,0:T(8,128)S(1)} %get-tuple-element.348, pred[512]{0:T(512)(128)(4,1)S(1)} %add_compare_fusion.2, ...), kind=kOutput, calls=%fused_computation.10.clone.1 | convolution fusion | flops 1097859072 | bytes 26280448 | tf_op jit(solution)/shard_map/cond/branch_1_fun/while/body/eval_jaxpr/hqk,khd->qhd/dot_general | solution.py:74
  302.4 11.5 %bitcast_reduce_fusion.2 = (f32[8,1024]{1,0:T(8,128)S(1)}, f32[8,512,1024]{2,1,0:T(8,128)}) fusion(pred[512]{0:T(512)(128)(4,1)S(1)} %add_compare_fusion.2, bf16[512,8,128]{0,2,1:T(8,128)(2,1)} %bitcast.71, bf16[1024,8,128]{2,0,1:T(8,128)(2,1)} %get-tuple-element.353), kind=kOutput, calls=%fused_computation.1.clone.1 | convolution fusion | flops 1086316544 | bytes 19956224 | tf_op jit(solution)/shard_map/cond/branch_1_fun/while/body/eval_jaxpr/qhd,khd->hqk/dot_general | solution.py:65
  313.9 8.2 %fusion.37 = f32[8,1024]{1,0:T(8,128)S(1)} fusion(f32[8,512,1024]{2,1,0:T(8,128)} %get-tuple-element.320, f32[8,1024]{1,0:T(8,128)S(1)} %get-tuple-element.348, pred[512]{0:T(512)(128)(4,1)S(1)} %add_compare_fusion.2), kind=kLoop, calls=%fused_computation.6.clone.1 | loop fusion | flops 20963328 | bytes 16843264 | tf_op jit(solution)/shard_map/cond/branch_1_fun/while/body/eval_jaxpr/reduce_sum | solution.py:73
  324.0 11.8 %bitcast_add_fusion.2 = f32[1024,8,128]{0,2,1:T(8,128)} fusion(f32[1024,8,128]{0,2,1:T(8,128)} %get-tuple-element.338, bf16[512,8,128]{0,2,1:T(8,128)(2,1)S(1)} %bitcast.72, f32[8,512,1024]{2,1,0:T(8,128)} %get-tuple-element.320, f32[8,1024]{1,0:T(8,128)S(1)} %get-tuple-element.348, pred[512]{0:T(512)(128)(4,1)S(1)} %add_compare_fusion.2, ...), kind=kOutput, calls=%fused_computation.10.clone.1 | convolution fusion | flops 1097859072 | bytes 26280448 | tf_op jit(solution)/shard_map/cond/branch_1_fun/while/body/eval_jaxpr/hqk,khd->qhd/dot_general | solution.py:74
  339.0 11.5 %bitcast_reduce_fusion.2 = (f32[8,1024]{1,0:T(8,128)S(1)}, f32[8,512,1024]{2,1,0:T(8,128)}) fusion(pred[512]{0:T(512)(128)(4,1)S(1)} %add_compare_fusion.2, bf16[512,8,128]{0,2,1:T(8,128)(2,1)} %bitcast.71, bf16[1024,8,128]{2,0,1:T(8,128)(2,1)} %get-tuple-element.353), kind=kOutput, calls=%fused_computation.1.clone.1 | convolution fusion | flops 1086316544 | bytes 19956224 | tf_op jit(solution)/shard_map/cond/branch_1_fun/while/body/eval_jaxpr/qhd,khd->hqk/dot_general | solution.py:65
  350.4 8.2 %fusion.37 = f32[8,1024]{1,0:T(8,128)S(1)} fusion(f32[8,512,1024]{2,1,0:T(8,128)} %get-tuple-element.320, f32[8,1024]{1,0:T(8,128)S(1)} %get-tuple-element.348, pred[512]{0:T(512)(128)(4,1)S(1)} %add_compare_fusion.2), kind=kLoop, calls=%fused_computation.6.clone.1 | loop fusion | flops 20963328 | bytes 16843264 | tf_op jit(solution)/shard_map/cond/branch_1_fun/while/body/eval_jaxpr/reduce_sum | solution.py:73
  360.6 11.8 %bitcast_add_fusion.2 = f32[1024,8,128]{0,2,1:T(8,128)} fusion(f32[1024,8,128]{0,2,1:T(8,128)} %get-tuple-element.338, bf16[512,8,128]{0,2,1:T(8,128)(2,1)S(1)} %bitcast.72, f32[8,512,1024]{2,1,0:T(8,128)} %get-tuple-element.320, f32[8,1024]{1,0:T(8,128)S(1)} %get-tuple-element.348, pred[512]{0:T(512)(128)(4,1)S(1)} %add_compare_fusion.2, ...), kind=kOutput, calls=%fused_computation.10.clone.1 | convolution fusion | flops 1097859072 | bytes 26280448 | tf_op jit(solution)/shard_map/cond/branch_1_fun/while/body/eval_jaxpr/hqk,khd->qhd/dot_general | solution.py:74
  375.5 11.5 %bitcast_reduce_fusion.2 = (f32[8,1024]{1,0:T(8,128)S(1)}, f32[8,512,1024]{2,1,0:T(8,128)}) fusion(pred[512]{0:T(512)(128)(4,1)S(1)} %add_compare_fusion.2, bf16[512,8,128]{0,2,1:T(8,128)(2,1)} %bitcast.71, bf16[1024,8,128]{2,0,1:T(8,128)(2,1)} %get-tuple-element.353), kind=kOutput, calls=%fused_computation.1.clone.1 | convolution fusion | flops 1086316544 | bytes 19956224 | tf_op jit(solution)/shard_map/cond/branch_1_fun/while/body/eval_jaxpr/qhd,khd->hqk/dot_general | solution.py:65
  387.0 8.2 %fusion.37 = f32[8,1024]{1,0:T(8,128)S(1)} fusion(f32[8,512,1024]{2,1,0:T(8,128)} %get-tuple-element.320, f32[8,1024]{1,0:T(8,128)S(1)} %get-tuple-element.348, pred[512]{0:T(512)(128)(4,1)S(1)} %add_compare_fusion.2), kind=kLoop, calls=%fused_computation.6.clone.1 | loop fusion | flops 20963328 | bytes 16843264 | tf_op jit(solution)/shard_map/cond/branch_1_fun/while/body/eval_jaxpr/reduce_sum | solution.py:73
  397.2 11.8 %bitcast_add_fusion.2 = f32[1024,8,128]{0,2,1:T(8,128)} fusion(f32[1024,8,128]{0,2,1:T(8,128)} %get-tuple-element.338, bf16[512,8,128]{0,2,1:T(8,128)(2,1)S(1)} %bitcast.72, f32[8,512,1024]{2,1,0:T(8,128)} %get-tuple-element.320, f32[8,1024]{1,0:T(8,128)S(1)} %get-tuple-element.348, pred[512]{0:T(512)(128)(4,1)S(1)} %add_compare_fusion.2, ...), kind=kOutput, calls=%fused_computation.10.clone.1 | convolution fusion | flops 1097859072 | bytes 26280448 | tf_op jit(solution)/shard_map/cond/branch_1_fun/while/body/eval_jaxpr/hqk,khd->qhd/dot_general | solution.py:74
  412.1 11.5 %bitcast_reduce_fusion.2 = (f32[8,1024]{1,0:T(8,128)S(1)}, f32[8,512,1024]{2,1,0:T(8,128)}) fusion(pred[512]{0:T(512)(128)(4,1)S(1)} %add_compare_fusion.2, bf16[512,8,128]{0,2,1:T(8,128)(2,1)} %bitcast.71, bf16[1024,8,128]{2,0,1:T(8,128)(2,1)} %get-tuple-element.353), kind=kOutput, calls=%fused_computation.1.clone.1 | convolution fusion | flops 1086316544 | bytes 19956224 | tf_op jit(solution)/shard_map/cond/branch_1_fun/while/body/eval_jaxpr/qhd,khd->hqk/dot_general | solution.py:65
  423.6 8.2 %fusion.37 = f32[8,1024]{1,0:T(8,128)S(1)} fusion(f32[8,512,1024]{2,1,0:T(8,128)} %get-tuple-element.320, f32[8,1024]{1,0:T(8,128)S(1)} %get-tuple-element.348, pred[512]{0:T(512)(128)(4,1)S(1)} %add_compare_fusion.2), kind=kLoop, calls=%fused_computation.6.clone.1 | loop fusion | flops 20963328 | bytes 16843264 | tf_op jit(solution)/shard_map/cond/branch_1_fun/while/body/eval_jaxpr/reduce_sum | solution.py:73
  433.8 11.8 %bitcast_add_fusion.2 = f32[1024,8,128]{0,2,1:T(8,128)} fusion(f32[1024,8,128]{0,2,1:T(8,128)} %get-tuple-element.338, bf16[512,8,128]{0,2,1:T(8,128)(2,1)S(1)} %bitcast.72, f32[8,512,1024]{2,1,0:T(8,128)} %get-tuple-element.320, f32[8,1024]{1,0:T(8,128)S(1)} %get-tuple-element.348, pred[512]{0:T(512)(128)(4,1)S(1)} %add_compare_fusion.2, ...), kind=kOutput, calls=%fused_computation.10.clone.1 | convolution fusion | flops 1097859072 | bytes 26280448 | tf_op jit(solution)/shard_map/cond/branch_1_fun/while/body/eval_jaxpr/hqk,khd->qhd/dot_general | solution.py:74
  448.7 11.5 %bitcast_reduce_fusion.2 = (f32[8,1024]{1,0:T(8,128)S(1)}, f32[8,512,1024]{2,1,0:T(8,128)}) fusion(pred[512]{0:T(512)(128)(4,1)S(1)} %add_compare_fusion.2, bf16[512,8,128]{0,2,1:T(8,128)(2,1)} %bitcast.71, bf16[1024,8,128]{2,0,1:T(8,128)(2,1)} %get-tuple-element.353), kind=kOutput, calls=%fused_computation.1.clone.1 | convolution fusion | flops 1086316544 | bytes 19956224 | tf_op jit(solution)/shard_map/cond/branch_1_fun/while/body/eval_jaxpr/qhd,khd->hqk/dot_general | solution.py:65
  460.2 8.2 %fusion.37 = f32[8,1024]{1,0:T(8,128)S(1)} fusion(f32[8,512,1024]{2,1,0:T(8,128)} %get-tuple-element.320, f32[8,1024]{1,0:T(8,128)S(1)} %get-tuple-element.348, pred[512]{0:T(512)(128)(4,1)S(1)} %add_compare_fusion.2), kind=kLoop, calls=%fused_computation.6.clone.1 | loop fusion | flops 20963328 | bytes 16843264 | tf_op jit(solution)/shard_map/cond/branch_1_fun/while/body/eval_jaxpr/reduce_sum | solution.py:73
  470.4 11.8 %bitcast_add_fusion.2 = f32[1024,8,128]{0,2,1:T(8,128)} fusion(f32[1024,8,128]{0,2,1:T(8,128)} %get-tuple-element.338, bf16[512,8,128]{0,2,1:T(8,128)(2,1)S(1)} %bitcast.72, f32[8,512,1024]{2,1,0:T(8,128)} %get-tuple-element.320, f32[8,1024]{1,0:T(8,128)S(1)} %get-tuple-element.348, pred[512]{0:T(512)(128)(4,1)S(1)} %add_compare_fusion.2, ...), kind=kOutput, calls=%fused_computation.10.clone.1 | convolution fusion | flops 1097859072 | bytes 26280448 | tf_op jit(solution)/shard_map/cond/branch_1_fun/while/body/eval_jaxpr/hqk,khd->qhd/dot_general | solution.py:74
  493.1 14.6 %collective-permute-done = bf16[1,256,1024]{2,1,0:T(8,128)(2,1)S(1)} collective-permute-done((bf16[1,256,1024]{2,1,0:T(8,128)(2,1)}, bf16[1,256,1024]{2,1,0:T(8,128)(2,1)S(1)}, u32[]{:S(2)}, u32[]{:S(2)}) %collective-permute-start) | collective-permute-done | bytes 524320 | tf_op jit(solution)/shard_map/ppermute | solution.py:29
  512.5 21.3 %collective-permute-done.1 = bf16[1,256,1024]{2,1,0:T(8,128)(2,1)} collective-permute-done((bf16[1,256,1024]{2,1,0:T(8,128)(2,1)}, bf16[1,256,1024]{2,1,0:T(8,128)(2,1)}, u32[]{:S(2)}, u32[]{:S(2)}) %collective-permute-start.1) | collective-permute-done | bytes 524320 | tf_op jit(solution)/shard_map/ppermute | solution.py:29
  537.4 5.4 copy.62
  (94 shorter events, 96.1 us)
Async XLA Ops:
  6.5 505.0 %copy-start = (f32[32,4096]{1,0:T(8,128)S(1)}, f32[32,4096]{1,0:T(8,128)}, u32[]{:S(2)}) copy-start(f32[32,4096]{1,0:T(8,128)} %param.13) | copy-start | bytes 1572868
  6.5 173.7 %all-gather.3.cloned.1.call-start = ((), (), s32[]{:S(2)}) async-start(), calls=%async_computation.3 | async-start | bytes 10485760 | tf_op jit(solution)/shard_map/all_gather | solution.py:52
  67.7 117.5 %all-gather.5.cloned.1.call-start = ((), (), s32[]{:S(2)}) async-start(), calls=%async_computation.4 | async-start | bytes 10485760 | tf_op jit(solution)/shard_map/all_gather | solution.py:53
  129.3 50.9 %all-to-all-start = ((bf16[256,4,1024]{0,2,1:T(8,128)(2,1)}), bf16[256,4,1024]{0,2,1:T(8,128)(2,1)S(1)}, u32[]{:S(2)}, u32[]{:S(2)}) async-start(bf16[256,4,1024]{0,2,1:T(8,128)(2,1)} %bitcast.76), calls=%async_computation | async-start | bytes 4194304 | tf_op jit(solution)/shard_map/all_to_all | solution.py:36
  487.8 23.1 %copy-start.1 = (s32[4]{0:T(128)S(1)}, s32[4]{0:T(128)}, u32[]{:S(2)}) copy-start(s32[4]{0:T(128)} %param.12) | copy-start | bytes 52
  491.6 16.1 %collective-permute-start = (bf16[1,256,1024]{2,1,0:T(8,128)(2,1)}, bf16[1,256,1024]{2,1,0:T(8,128)(2,1)S(1)}, u32[]{:S(2)}, u32[]{:S(2)}) collective-permute-start(bf16[1,256,1024]{2,1,0:T(8,128)(2,1)} %constant_dynamic-slice_fusion.4), channel_id=1, source_target_pairs={{0,1},{1,2},{2,3},{3,0},{4,5},{5,6},{6,7},{7,4},{8,9},{9,10},{10,1... | collective-permute-start | bytes 1572872 | tf_op jit(solution)/shard_map/ppermute | solution.py:29
  508.8 25.0 %collective-permute-start.1 = (bf16[1,256,1024]{2,1,0:T(8,128)(2,1)}, bf16[1,256,1024]{2,1,0:T(8,128)(2,1)}, u32[]{:S(2)}, u32[]{:S(2)}) collective-permute-start(bf16[1,256,1024]{2,1,0:T(8,128)(2,1)} %get-tuple-element.260), channel_id=1, source_target_pairs={{0,2},{1,3},{2,0},{3,1},{4,6},{5,7},{6,4},{7,5},{8,10},{9,11},{10,... | collective-permute-start | bytes 1572872 | tf_op jit(solution)/shard_map/ppermute | solution.py:29
  509.4 25.5 %collective-permute-start.2 = (bf16[1,256,1024]{2,1,0:T(8,128)(2,1)}, bf16[1,256,1024]{2,1,0:T(8,128)(2,1)S(1)}, u32[]{:S(2)}, u32[]{:S(2)}) collective-permute-start(bf16[1,256,1024]{2,1,0:T(8,128)(2,1)} %get-tuple-element.259), channel_id=1, source_target_pairs={{0,3},{1,0},{2,1},{3,2},{4,7},{5,4},{6,5},{7,6},{8,11},{9,8},{10,9... | collective-permute-start | bytes 1572872 | tf_op jit(solution)/shard_map/ppermute | solution.py:29
Sparse Core Ops, SparseCore 0:
  67.8 57.4 all-gather.2
  126.9 58.2 all-gather.4
